TPU v7x, 32 devices: a whole 2x2x4 slice. The times are simulated.
32 devices in a mesh: groups: 2 (over x), tile: 8 (over z, y), example: 2 (over core).
Axes of the slice: x: 2, y: 2, z: 4, core: 2. Of those that a mesh axis runs over, the one named last changes fastest.
Arguments:
- features: bfloat16 [4096, 8192], P(('groups', 'example'), 'tile'), parts along dimension 0
- tile_lists: int32 [272, 3], P('groups'), parts along dimension 0, may hold values from 0 to 15, as said below
- noise_tiles: float32 [544, 512, 512], P(('groups', 'tile'), 'example'), parts along dimension 0, may hold values from -6 to 6
Outputs:
- covariance: float32 [544, 512, 512], P(('groups', 'tile'), 'example'), parts along dimension 0
There are 2 independent parts, one for each index of `groups`. A program takes and returns all parts, laid end to end along the dimension named above; each array names one. Nothing has to cross between parts.
Inputs may be any that keep to these rules, and one draw needn't show every extreme that they name: `tile_lists`: every tile (i, j) with 0 <= j <= i < 16 appears once, in an order drawn from the seed; owners lie in 0 to 7, no owner has more than 34 tiles and some owner has exactly 34.
All inputs are finite; a program needn't handle non-finite values.
Results may differ from a plain program's by a relative error of at most 0.0023.
Values may be sent and summed in bfloat16 or wider, within the bound.
No kernel may reach another device: no remote copies, remote signals or barrier semaphores. Data moves between devices by JAX's collectives and lax.ppermute only.
A program may use at most 192 MiB of HBM per device.

v0:
```python
import math

import jax
import jax.numpy as jnp
from jax import lax
from jax.sharding import PartitionSpec as P

F = 8192


def slot_table(tile_lists, owner, slots):
    owners = tile_lists[:, 2]
    entries = tile_lists.shape[0]
    position = jnp.arange(entries, dtype=jnp.int32)
    mine = owners == owner
    earlier = (position[None, :] < position[:, None]) & mine[None, :]
    ranks = jnp.sum(earlier.astype(jnp.int32), axis=1)
    matches = (
        mine[None, :] & (ranks[None, :] == jnp.arange(slots, dtype=jnp.int32)[:, None])
    ).astype(jnp.int32)
    living = jnp.sum(matches, axis=1)
    first = jnp.sum(matches * tile_lists[None, :, 0], axis=1)
    second = jnp.sum(matches * tile_lists[None, :, 1], axis=1)
    return (first, second, living)


def tile_product(wide, first, second, offset, height, stripe):
    left = lax.dynamic_slice_in_dim(wide, first * stripe + offset, height, 1)
    right = lax.dynamic_slice_in_dim(wide, second * stripe, stripe, 1)
    return jnp.dot(left.T, right, preferred_element_type=jnp.float32)


def body(features, tile_lists, noise_tiles):
    slots, height, stripe = noise_tiles.shape
    values = features.astype(jnp.float32)
    squares = jnp.sum(values * values, axis=1)
    norms = lax.psum(squares, "tile")
    inverse = 1.0 / jnp.maximum(jnp.sqrt(norms), math.sqrt(2.0 * F))
    scaled = (values * inverse[:, None]).astype(jnp.bfloat16)
    owner = lax.axis_index("tile")
    first, second, living = slot_table(tile_lists, owner, slots)
    cov_scale = F / math.sqrt(features.shape[0] * lax.axis_size("example"))
    wide = lax.all_gather(scaled, "tile", axis=1, tiled=True)

    def partial_tile(entry):
        one, two, alive = entry
        return lax.cond(
            alive > 0,
            lambda: tile_product(wide, one, two, 0, stripe, stripe),
            lambda: jnp.zeros((stripe, stripe), jnp.float32),
        )

    partials = lax.map(partial_tile, (first, second, living))
    summed = lax.psum_scatter(partials, "example", scatter_dimension=1, tiled=True)
    return jnp.where(living[:, None, None] > 0, cov_scale * summed + noise_tiles, 0.0)


def solution(mesh):
    placed = (
        P(("groups", "example"), "tile"),
        P("groups", None),
        P(("groups", "tile"), "example", None),
    )
    return jax.shard_map(
        body,
        mesh=mesh,
        in_specs=placed,
        out_specs=P(("groups", "tile"), "example", None),
        check_vma=False,
    )
```

profile of v0, /device:TPU:5, one launch (start us, length us, event | category | flops | bytes accessed | tf_op | source)
XLA Modules:
  0.0 566.9 jit_solution(10095957913680222901)
XLA Ops:
  8.6 14.4 %psum.7 = f32[1024]{0:T(1024)S(1)} all-reduce(f32[1024]{0:T(1024)S(1)} %fusion.3), channel_id=1, replica_groups=mesh['groups'=2,'tile'=8,'example'=2] {'tile'}, use_global_device_ids=true, to_apply=%region_5.0 | all-reduce | flops 1024 | bytes 8192 | tf_op jit(solution)/shard_map/psum | solution.py:37
  23.1 3.3 fusion.4
  28.2 229.1 %all-gather.2.cloned.1.call-done = bf16[1024,8192]{1,0:T(8,128)(2,1)} async-done(((bf16[1024,1024]{1,0:T(8,128)(2,1)}), bf16[1024,8192]{1,0:T(8,128)(2,1)}) %all-gather.2.cloned.1.call-update) | async-done | bytes 16777232 | tf_op jit(solution)/shard_map/all_gather | solution.py:43
  257.3 187.5 %while.10 = (s32[]{:T(128)}, f32[34,512,512]{2,1,0:T(8,128)}, s32[34]{0:T(128)S(1)}, s32[34]{0:T(128)S(1)}, bf16[1024,8192]{1,0:T(8,128)(2,1)}, /*index=5*/s32[34]{0:T(128)S(1)}, s32[]{:T(128)}, s32[1]{0:T(128)}) while((s32[]{:T(128)}, f32[34,512,512]{2,1,0:T(8,128)}, s32[34]{0:T(128)S(1)}, s32[34]{0:T(128)S(1)}, ...), condition=%wide.region_9.10_spmd, body=%wide.region_6.9_spmd.sunk | while | flops 536870912 | bytes 5243667 | solution.py:53
  258.5 4.7 conditional.2
  265.5 4.7 conditional.2
  272.5 4.7 conditional.2
  279.5 4.7 conditional.2
  286.4 4.7 conditional.2
  293.4 4.7 conditional.2
  300.4 4.7 conditional.2
  307.4 4.7 conditional.2
  314.4 4.7 conditional.2
  321.4 4.7 conditional.2
  323.8 2.3 convolution_bitcast_fusion
  328.4 4.7 conditional.2
  335.3 4.7 conditional.2
  342.3 4.7 conditional.2
  344.7 2.3 convolution_bitcast_fusion
  349.3 4.7 conditional.2
  356.3 4.7 conditional.2
  363.2 4.7 conditional.2
  370.2 4.7 conditional.2
  377.2 4.7 conditional.2
  384.2 4.7 conditional.2
  391.2 4.7 conditional.2
  398.2 4.7 conditional.2
  405.1 4.7 conditional.2
  407.5 2.3 convolution_bitcast_fusion
  412.2 4.7 conditional.2
  444.9 97.0 %reduce-scatter.2.cloned.1.call-done = f32[34,256,512]{2,1,0:T(8,128)} async-done(((f32[34,512,512]{2,1,0:T(8,128)}), f32[34,256,512]{2,1,0:T(8,128)}) %reduce-scatter.2.cloned.1.call-update) | async-done | bytes 17825808 | tf_op jit(solution)/shard_map/reduce_scatter | solution.py:54
  541.9 18.2 %add_select_fusion = f32[34,256,512]{2,1,0:T(8,128)} fusion(f32[34,256,512]{2,1,0:T(8,128)} %param.9, f32[34,256,512]{2,1,0:T(8,128)} %reduce-scatter.2.cloned.1.call-done, pred[34]{0:T(512)(128)(4,1)S(1)} %broadcast_compare_fusion), kind=kLoop, calls=%fused_computation.5 | loop fusion | flops 13369344 | bytes 53477408 | tf_op jit(solution)/shard_map/jit(_where)/select_n | solution.py:55
  (168 shorter events, 136.0 us)
Async XLA Ops:
  6.5 250.8 %all-gather.2.cloned.1.call-start = ((), (), s32[]{:S(2)}) async-start(), calls=%async_computation.1 | async-start | bytes 18874368 | tf_op jit(solution)/shard_map/all_gather | solution.py:43
  26.4 515.5 %reduce-scatter.2.cloned.1.call-start = ((), (), s32[]{:S(2)}) async-start(), calls=%async_computation.2 | async-start | bytes 53477376 | tf_op jit(solution)/shard_map/reduce_scatter | solution.py:54
Sparse Core Ops, SparseCore 0:
  26.5 230.7 all-gather.1
  445.0 96.8 reduce-scatter.1
where the time goes:
time: 570 us; the launch traced here: 567 us
  waiting for transfers between devices  326 us (57%)
  local copies, waits for them, and re-layouts  85.7 us (15%)
  matrix products  52.6 us (9%)
  loops' own time  50.1 us (9%)
  other arithmetic  24.6 us (4%)
  blocking collectives  14.4 us (3%)
  between operations  13.4 us (2%)
    all_gather x1, waiting for transfers between devices, body(): wide = lax.all_gather(scaled, 'tile', axis=1, tiled=True)  229 us
    reduce_scatter x1, waiting for transfers between devices, body(): lax.psum_scatter(partials, 'example', scatter_dimension=1, tiled=True)  97 us
    dot_general x23, matrix products, tile_product(): return jnp.dot(left.T, right, preferred_element_type=jnp.float32)  52.6 us
    dynamic_slice x80, local copies, waits for them, and re-layouts, body(): partials = lax.map(partial_tile, (first, second, living))  47.2 us
    dynamic_update_slice x34, local copies, waits for them, and re-layouts, body(): partials = lax.map(partial_tile, (first, second, living))  36.4 us
    another operation x34, loops' own time, partial_tile(): lax.cond(alive > 0, lambda: tile_product(wide, one, two, 0, stripe, strip...  27.6 us
    another operation x1, loops' own time, body(): partials = lax.map(partial_tile, (first, second, living))  22.4 us
    select_n x1, other arithmetic, body(): jnp.where(living[:, None, None] > 0, cov_scale * summed + noise_tiles, 0.0)  18.2 us
  transfers between devices with their start and end apart: 2, of which 2 were waited for; matrix products, arithmetic and copies ran while one was open for 0% of the time, Pallas kernels for 0%

commit v1 on v0

v1 whole, which is shorter than its diff:
```python
import functools
import math

import jax
import jax.numpy as jnp
import numpy as np
from jax import lax
from jax.experimental import pallas as pl
from jax.experimental.pallas import tpu as pltpu
from jax.sharding import PartitionSpec as P

F = 8192
VMEM = 48 * 1024 * 1024
CORES = [(0, 1), (1, 0)]

Y_SWAP = [(2 * z + y, 2 * z + 1 - y) for z in range(4) for y in range(2)]
Z_SWAP = [(2 * a + y, 2 * b + y) for a, b in ((0, 1), (1, 0), (2, 3), (3, 2)) for y in range(2)]
M_SWAP = [(2 * a + y, 2 * b + y) for a, b in ((1, 2), (2, 1)) for y in range(2)]


def slot_table(tile_lists, owner, slots):
    owners = tile_lists[:, 2]
    entries = tile_lists.shape[0]
    position = jnp.arange(entries, dtype=jnp.int32)
    mine = owners == owner
    earlier = (position[None, :] < position[:, None]) & mine[None, :]
    ranks = jnp.sum(earlier.astype(jnp.int32), axis=1)
    matches = (
        mine[None, :] & (ranks[None, :] == jnp.arange(slots, dtype=jnp.int32)[:, None])
    ).astype(jnp.int32)
    living = jnp.sum(matches, axis=1)
    first = jnp.sum(matches * tile_lists[None, :, 0], axis=1)
    second = jnp.sum(matches * tile_lists[None, :, 1], axis=1)
    return (first, second, living)


def arrivals():
    held = {}
    for z in range(4):
        for y in range(2):
            a = lambda plane, half: 2 * (2 * plane + y) + half
            o = lambda plane, half: 2 * (2 * plane + 1 - y) + half
            if z in (0, 3):
                near = 1 if z == 0 else 2
                over, far = 3 - near, 3 - z
                zs = [a(near, 0), a(near, 1), a(over, 0), a(over, 1), a(far, 0), a(far, 1), o(far, 1)]
                ys = [o(z, 0), o(z, 1), o(near, 0), o(near, 1), o(over, 0), o(over, 1), o(far, 0)]
                ms = [-1] * 4
            else:
                edge = 0 if z == 1 else 3
                over, far = 3 - z, 3 - edge
                zs = [a(edge, 0), a(edge, 1), o(edge, 0), o(edge, 1), -1, -1, -1]
                ys = [o(z, 0), o(z, 1), o(over, 0), o(over, 1), o(far, 0), o(far, 1), -1]
                ms = [a(over, 0), a(over, 1), a(far, 0), a(far, 1)]
            row = {"own0": a(z, 0), "own1": a(z, 1)}
            row.update({f"z{k + 1}": s for k, s in enumerate(zs)})
            row.update({f"y{k + 1}": s for k, s in enumerate(ys)})
            row.update({f"m{k + 1}": s for k, s in enumerate(ms)})
            held[2 * z + y] = row
    return held


STAGES = (
    ("own0", "own1", "z1", "y1", "m1", "z2", "y2", "m2"),
    ("z3", "y3", "m3", "z4", "y4", "m4"),
    ("z5", "y5"),
    ("z6", "y6"),
    ("z7", "y7"),
)


def prep_kernel(meta, mine, other, inv_mine, inv_other, *rest):
    right, left = rest[-2:]
    half = pl.program_id(0)
    width = left.shape[1]
    columns = pl.ds(pl.multiple_of(meta[1] * width, width), width)

    def scale(raw, inv):
        right[0] = (raw[...].astype(jnp.float32) * inv[...]).astype(jnp.bfloat16)
        part = raw[:, columns].astype(jnp.float32) * inv[...]
        left[0] = part.T.astype(jnp.bfloat16)

    @pl.when(half == 0)
    def _():
        scale(mine, inv_mine)

    @pl.when(half == 1)
    def _():
        scale(other, inv_other)


def prepare(meta, mine, other, inv_mine, inv_other, held, after, stripes, height):
    rows, stripe = mine.shape
    chunk = 512
    steps = rows // chunk
    raw = lambda want: pl.BlockSpec(
        (chunk, stripe), lambda h, r, m: (jnp.where(h == want, r, 0 if want else steps - 1), 0)
    )
    inv = lambda want: pl.BlockSpec(
        (chunk, 1), lambda h, r, m: (jnp.where(h == want, r, 0 if want else steps - 1), 0)
    )
    anywhere = pl.BlockSpec(memory_space=pl.ANY)
    extra = [] if held is None else [*held, *after]
    return pl.pallas_call(
        prep_kernel,
        grid_spec=pltpu.PrefetchScalarGridSpec(
            num_scalar_prefetch=1,
            grid=(2, steps),
            in_specs=[raw(0), raw(1), inv(0), inv(1)] + [anywhere] * len(extra),
            out_specs=[
                pl.BlockSpec((1, chunk, stripe), lambda h, r, m: (m[0], h * steps + r, 0)),
                pl.BlockSpec((1, height, chunk), lambda h, r, m: (m[0], 0, h * steps + r)),
            ],
        ),
        out_shape=[
            jax.ShapeDtypeStruct((stripes + 1, 2 * rows, stripe), jnp.bfloat16),
            jax.ShapeDtypeStruct((stripes + 1, height, 2 * rows), jnp.bfloat16),
        ],
        input_output_aliases={} if held is None else {5: 0, 6: 1},
        compiler_params=pltpu.CompilerParams(vmem_limit_bytes=VMEM),
        cost_estimate=pl.CostEstimate(flops=4 * rows * stripe, bytes_accessed=10 * rows * stripe, transcendentals=0),
        name="prepare",
    )(meta, mine, other, inv_mine, inv_other, *extra)


def gram_kernel(cov_scale, stage, lefts, rights, slots, steps, span, left, right, noise, *rest):
    out = rest[-1]
    _, height, stripe = out.shape
    depth = right.shape[1]
    start = span[0]

    def one_tile(l, r, n, o):
        e = start + pl.program_id(0)
        alive = (steps[e] >= 0) & (steps[e] <= stage)

        @pl.when(alive)
        def _():
            gram = jnp.dot(l[0], r[0], preferred_element_type=jnp.float32)
            o[0] = cov_scale * gram + n[0]

        @pl.when(jnp.logical_not(alive))
        def _():
            o[0] = jnp.zeros_like(o[0])

    pltpu.emit_pipeline(
        one_tile,
        grid=(span[1],),
        in_specs=[
            pl.BlockSpec((1, height, depth), lambda e: (lefts[start + e], 0, 0)),
            pl.BlockSpec((1, depth, stripe), lambda e: (rights[start + e], 0, 0)),
            pl.BlockSpec((1, height, stripe), lambda e: (slots[start + e], 0, 0)),
        ],
        out_specs=[pl.BlockSpec((1, height, stripe), lambda e: (slots[start + e], 0, 0))],
    )(left, right, noise, out)


def grams(cov_scale, stage, table, span, right, left, noise, out):
    slots, height, stripe = noise.shape
    depth = right.shape[1]
    extra = [] if out is None else [out]
    anywhere = pl.BlockSpec(memory_space=pl.ANY)
    return pl.pallas_call(
        functools.partial(gram_kernel, cov_scale, stage),
        in_specs=[pl.BlockSpec(memory_space=pltpu.SMEM)] * 5 + [anywhere] * (3 + len(extra)),
        out_specs=anywhere,
        out_shape=jax.ShapeDtypeStruct(noise.shape, jnp.float32),
        input_output_aliases={} if out is None else {8: 0},
        compiler_params=pltpu.CompilerParams(vmem_limit_bytes=VMEM),
        cost_estimate=pl.CostEstimate(
            flops=2 * 8 * height * stripe * depth, bytes_accessed=8 * 4 * 1024 * 1024, transcendentals=0
        ),
        name="grams",
    )(*table, span, left, right, noise, *extra)


def schedule(first, second, living, stage_of, stages):
    slots = first.shape[0]
    look = lambda index: jnp.sum(
        jnp.where(index[:, None] == jnp.arange(stage_of.shape[0])[None, :], stage_of[None, :], 0), axis=1
    )
    stage = jnp.where(living > 0, jnp.maximum(look(first), look(second)), -1)
    position = jnp.arange(slots, dtype=jnp.int32)
    key = (((stage + 1) * 64 + second) * 64 + first) * slots + position
    rank = jnp.sum((key[None, :] < key[:, None]).astype(jnp.int32), axis=1)
    pick = (rank[None, :] == position[:, None]).astype(jnp.int32)
    put = lambda values: jnp.sum(pick * values[None, :], axis=1)
    table = (put(first), put(second), put(position), put(stage))
    spans, begin = [], jnp.int32(0)
    for step in range(stages):
        end = jnp.sum((stage <= step).astype(jnp.int32))
        count = end - begin
        start = jnp.where(count > 0, begin, slots - 1)
        spans.append(jnp.stack([start, jnp.maximum(count, 1)]).astype(jnp.int32))
        begin = end
    return table, spans


def grid_body(features, tile_lists, noise_tiles):
    slots, height, stripe = noise_tiles.shape
    rows = features.shape[0]
    chips = lax.axis_size("tile")
    stripes = features.shape[1] * chips // stripe
    chip = lax.axis_index("tile")
    core = lax.axis_index("example")
    at_end = (chip < 2) | (chip >= chips - 2)
    cov_scale = F / math.sqrt(rows * lax.axis_size("example"))
    y = lambda x: lax.ppermute(x, "tile", Y_SWAP)
    z = lambda x: lax.ppermute(x, "tile", Z_SWAP)
    m = lambda x: lax.ppermute(x, "tile", M_SWAP)
    pick = lambda a, b: jnp.where(at_end, a, b)

    b = {"own0": features[:, :stripe], "own1": features[:, stripe:]}
    for k in (1, 2):
        own = b[f"own{k - 1}"]
        b[f"y{k}"], b[f"z{k}"], b[f"m{k}"] = y(own), z(own), m(own)
    for k in (3, 4):
        near_z, near_m, near_y = b[f"z{k - 2}"], b[f"m{k - 2}"], b[f"y{k - 2}"]
        b[f"y{k}"] = y(pick(near_z, near_m))
        b[f"z{k}"] = z(pick(near_y, near_m))
        b[f"m{k}"] = m(near_z)
    for k in (5, 6):
        near_z, near_m = b[f"z{k - 2}"], b[f"m{k - 2}"]
        b[f"y{k}"] = y(pick(near_z, near_m))
        b[f"z{k}"] = z(near_m)
    b["y7"] = y(b["z5"])
    b["z7"] = z(b["y6"])

    values = features.astype(jnp.float32)
    norms = lax.psum(jnp.sum(values * values, axis=1), "tile")
    inverse = (1.0 / jnp.maximum(jnp.sqrt(norms), math.sqrt(2.0 * F)))[:, None]
    inverse_other = lax.ppermute(inverse, "example", CORES)

    held_at = arrivals()
    stage_of = np.zeros((chips, stripes), np.int32)
    for c in range(chips):
        for s, names in enumerate(STAGES):
            for n in names:
                if held_at[c][n] >= 0:
                    stage_of[c, held_at[c][n]] = s
    first, second, living = slot_table(tile_lists, chip, slots)
    table, spans = schedule(first, second, living, jnp.asarray(stage_of)[chip], len(STAGES))

    held, out = None, None
    for s, names in enumerate(STAGES):
        for n in names:
            place = jnp.asarray([held_at[c][n] if held_at[c][n] >= 0 else stripes for c in range(chips)], jnp.int32)
            meta = jnp.stack([place[chip], core])
            other = lax.ppermute(b[n], "example", CORES)
            after = [] if out is None else [out]
            held = prepare(meta, b[n], other, inverse, inverse_other, held, after, stripes, height)
        out = grams(cov_scale, s, table, spans[s], *held, noise_tiles, out)
    return out


def plain_body(features, tile_lists, noise_tiles):
    slots, height, stripe = noise_tiles.shape
    rows = features.shape[0]
    chips = lax.axis_size("tile")
    stripes = features.shape[1] * chips // stripe
    core = lax.axis_index("example")
    cov_scale = F / math.sqrt(rows * lax.axis_size("example"))
    values = features.astype(jnp.float32)
    norms = lax.psum(jnp.sum(values * values, axis=1), "tile")
    inverse = (1.0 / jnp.maximum(jnp.sqrt(norms), math.sqrt(2.0 * F)))[:, None]
    scaled = (values * inverse).astype(jnp.bfloat16)
    wide = lax.all_gather(lax.all_gather(scaled, "tile", axis=1, tiled=True), "example", axis=0, tiled=True)
    right = wide.reshape(2 * rows, stripes, stripe).transpose(1, 0, 2)
    left = lax.dynamic_slice_in_dim(right, core * height, height, 2).transpose(0, 2, 1)
    first, second, living = slot_table(tile_lists, lax.axis_index("tile"), slots)
    table, spans = schedule(first, second, living, jnp.zeros((stripes,), jnp.int32), 1)
    return grams(cov_scale, 0, table, spans[0], right, left, noise_tiles, None)


def body(features, tile_lists, noise_tiles):
    if lax.axis_size("tile") == 8 and features.shape[1] == 2 * noise_tiles.shape[2]:
        return grid_body(features, tile_lists, noise_tiles)
    return plain_body(features, tile_lists, noise_tiles)


def solution(mesh):
    placed = (
        P(("groups", "example"), "tile"),
        P("groups", None),
        P(("groups", "tile"), "example", None),
    )
    return jax.shard_map(
        body,
        mesh=mesh,
        in_specs=placed,
        out_specs=P(("groups", "tile"), "example", None),
        check_vma=False,
    )
```

time: 570 us -> 366 us (0.64)
  the two profiles are of different devices: /device:TPU:5 before, /device:TPU:7 now
where the time goes in v1:
time: 366 us; the launch traced here: 362 us
  Pallas kernels  153 us (42%)
  waiting for transfers between devices  59.9 us (16%)
  starting transfers between devices  49.5 us (14%)
  local copies, waits for them, and re-layouts  35.8 us (10%)
  blocking collectives  31 us (8%)
  other arithmetic  23.9 us (7%)
  between operations  8.89 us (2%)
    pallas_call x20, Pallas kernels, prepare(): pl.pallas_call(prep_kernel, grid_spec=pltpu.PrefetchScalarGridSpec(num_sc...  93.7 us
    pallas_call x5, Pallas kernels, grams(): pl.pallas_call(functools.partial(gram_kernel, cov_scale, stage), in_specs...  59.8 us
    ppermute x7, waiting for transfers between devices, grid_body(): z = lambda x: lax.ppermute(x, 'tile', Z_SWAP)  42.4 us
    psum x1, blocking collectives, grid_body(): norms = lax.psum(jnp.sum(values * values, axis=1), 'tile')  31 us
    dynamic_slice x19, local copies, waits for them, and re-layouts, grid_body(): meta = jnp.stack([place[chip], core])  23.3 us
    ppermute x7, starting transfers between devices, grid_body(): z = lambda x: lax.ppermute(x, 'tile', Z_SWAP)  18.4 us
    ppermute x20, starting transfers between devices, grid_body(): other = lax.ppermute(b[n], 'example', CORES)  17.4 us
    ppermute x7, waiting for transfers between devices, grid_body(): y = lambda x: lax.ppermute(x, 'tile', Y_SWAP)  15.9 us
  transfers between devices with their start and end apart: 39, of which 7 were waited for; matrix products, arithmetic and copies ran while one was open for 13% of the time, Pallas kernels for 37%

profile of v1, /device:TPU:7, one launch (start us, length us, event | category | flops | bytes accessed | tf_op | source)
XLA Modules:
  0.0 362.5 jit_solution(1024040790887599413)
XLA Ops:
  6.9 31.0 %psum.7 = f32[1024]{0:T(1024)S(1)} all-reduce(f32[1024]{0:T(1024)S(1)} %multiply_reduce_fusion), channel_id=1, replica_groups=mesh['groups'=2,'tile'=8,'example'=2] {'tile'}, use_global_device_ids=true, to_apply=%region_14.15 | all-reduce | flops 1024 | bytes 8192 | tf_op jit(solution)/shard_map/psum | solution.py:229
  38.2 4.3 %collective-permute-start.5 = (f32[1024,1]{1,0:T(8,128)S(1)}, f32[1024,1]{1,0:T(8,128)S(1)}, u32[]{:S(2)}, u32[]{:S(2)}) collective-permute-start(f32[1024,1]{1,0:T(8,128)S(1)} %copy.108.inv_mine), channel_id=1, source_target_pairs={{0,1},{1,0},{2,3},{3,2},{4,5},{5,4},{6,7},{7,6},{8,9},{9,8},{10,11... | collective-permute-start | bytes 12296 | tf_op jit(solution)/shard_map/ppermute | solution.py:231
  49.7 20.5 %collective-permute-done.9.mine = bf16[1024,512]{1,0:T(8,128)(2,1)} collective-permute-done((bf16[1024,512]{1,0:T(8,128)(2,1)S(1)}, bf16[1024,512]{1,0:T(8,128)(2,1)}, u32[]{:S(2)}, u32[]{:S(2)}) %collective-permute-start.9) | collective-permute-done | bytes 1048608 | tf_op jit(solution)/shard_map/ppermute | solution.py:208
  86.8 8.8 %collective-permute-start.19 = (bf16[1024,512]{1,0:T(8,128)(2,1)S(1)}, bf16[1024,512]{1,0:T(8,128)(2,1)S(1)}, u32[]{:S(2)}, u32[]{:S(2)}) collective-permute-start(bf16[1024,512]{1,0:T(8,128)(2,1)S(1)} %get-tuple-element.103), channel_id=1, source_target_pairs={{0,4},{2,6},{4,0},{6,2},{8,12},{10,14},{12,8},{14,10},{1,5},{3,7},... | collective-permute-start | bytes 3145736 | tf_op jit(solution)/shard_map/ppermute | solution.py:208
  115.1 3.7 %collective-permute-done.19.mine = bf16[1024,512]{1,0:T(8,128)(2,1)S(1)} collective-permute-done((bf16[1024,512]{1,0:T(8,128)(2,1)S(1)}, bf16[1024,512]{1,0:T(8,128)(2,1)S(1)}, u32[]{:S(2)}, u32[]{:S(2)}) %collective-permute-start.19) | collective-permute-done | bytes 1048608 | tf_op jit(solution)/shard_map/ppermute | solution.py:208
  131.1 10.1 %collective-permute-done.8.mine = bf16[1024,512]{1,0:T(8,128)(2,1)S(1)} collective-permute-done((bf16[1024,512]{1,0:T(8,128)(2,1)S(1)}, bf16[1024,512]{1,0:T(8,128)(2,1)S(1)}, u32[]{:S(2)}, u32[]{:S(2)}) %collective-permute-start.8) | collective-permute-done | bytes 1048608 | tf_op jit(solution)/shard_map/ppermute | solution.py:208
  144.8 6.5 %collective-permute-start.2 = (bf16[1024,512]{1,0:T(8,128)(2,1)S(1)}, bf16[1024,512]{1,0:T(8,128)(2,1)}, u32[]{:S(2)}, u32[]{:S(2)}) collective-permute-start(bf16[1024,512]{1,0:T(8,128)(2,1)S(1)} %collective-permute-done.1.mine), channel_id=1, source_target_pairs={{0,4},{2,6},{4,0},{6,2},{8,12},{10,14},{12,8},{14,10},{1,5},{3,7},... | collective-permute-start | bytes 3145736 | tf_op jit(solution)/shard_map/ppermute | solution.py:208
  164.4 8.2 %collective-permute-done.2.mine = bf16[1024,512]{1,0:T(8,128)(2,1)} collective-permute-done((bf16[1024,512]{1,0:T(8,128)(2,1)S(1)}, bf16[1024,512]{1,0:T(8,128)(2,1)}, u32[]{:S(2)}, u32[]{:S(2)}) %collective-permute-start.2) | collective-permute-done | bytes 1048608 | tf_op jit(solution)/shard_map/ppermute | solution.py:208
  172.6 5.4 %collective-permute-start.22 = (bf16[1024,512]{1,0:T(8,128)(2,1)}, bf16[1024,512]{1,0:T(8,128)(2,1)}, u32[]{:S(2)}, u32[]{:S(2)}) collective-permute-start(bf16[1024,512]{1,0:T(8,128)(2,1)} %collective-permute-done.2.mine), channel_id=1, source_target_pairs={{0,1},{1,0},{2,3},{3,2},{4,5},{5,4},{6,7},{7,6},{8,9},{9,8},{10,11... | collective-permute-start | bytes 3145736 | tf_op jit(solution)/shard_map/ppermute | solution.py:248
  189.5 15.6 %collective-permute-done.20.mine = bf16[1024,512]{1,0:T(8,128)(2,1)} collective-permute-done((bf16[1024,512]{1,0:T(8,128)(2,1)}, bf16[1024,512]{1,0:T(8,128)(2,1)}, u32[]{:S(2)}, u32[]{:S(2)}) %collective-permute-start.20) | collective-permute-done | bytes 1048608 | tf_op jit(solution)/shard_map/ppermute | solution.py:207
  206.6 5.2 %prepare.20 = (bf16[17,2048,512]{2,1,0:T(8,128)(2,1)}, bf16[17,256,2048]{2,1,0:T(8,128)(2,1)}) custom-call(s32[2]{0:T(128)S(1)} %pad_add_fusion.20.meta, bf16[1024,512]{1,0:T(8,128)(2,1)} %get-tuple-element.101.mine, bf16[1024,512]{1,0:T(8,128)(2,1)} %collective-permute-done.38.other, f32[1024,1]{1,0:T(8,128)S(1)} %copy.108.inv_mine, ...), custom_call_target="tpu_custom_call" | custom-call | flops 2097152 | bytes 5242880 | tf_op jit(solution)/shard_map/prepare/pallas_call | solution.py:104
  213.1 5.1 %prepare.21 = (bf16[17,2048,512]{2,1,0:T(8,128)(2,1)}, bf16[17,256,2048]{2,1,0:T(8,128)(2,1)}) custom-call(s32[2]{0:T(128)S(1)} %pad_add_fusion.19.meta, bf16[1024,512]{1,0:T(8,128)(2,1)S(1)} %copy-done.7, bf16[1024,512]{1,0:T(8,128)(2,1)} %collective-permute-done.37.other, ...), custom_call_target="tpu_custom_call", output_to_operand_aliasing={{0}: (5, {}), {1}: (6, {})} | custom-call | flops 2097152 | bytes 5242880 | tf_op jit(solution)/shard_map/prepare/pallas_call | solution.py:104
  218.2 5.3 %prepare.22 = (bf16[17,2048,512]{2,1,0:T(8,128)(2,1)}, bf16[17,256,2048]{2,1,0:T(8,128)(2,1)}) custom-call(s32[2]{0:T(128)S(1)} %pad_add_fusion.18.meta, bf16[1024,512]{1,0:T(8,128)(2,1)} %collective-permute-done.mine, bf16[1024,512]{1,0:T(8,128)(2,1)} %collective-permute-done.36.other, ...), custom_call_target="tpu_custom_call", output_to_operand_aliasing={{0}: (5, {}), {1}: (6, {})} | custom-call | flops 2097152 | bytes 5242880 | tf_op jit(solution)/shard_map/prepare/pallas_call | solution.py:104
  223.5 5.1 %prepare.23 = (bf16[17,2048,512]{2,1,0:T(8,128)(2,1)}, bf16[17,256,2048]{2,1,0:T(8,128)(2,1)}) custom-call(s32[2]{0:T(128)S(1)} %pad_add_fusion.17.meta, bf16[1024,512]{1,0:T(8,128)(2,1)S(1)} %copy-done.5, bf16[1024,512]{1,0:T(8,128)(2,1)} %collective-permute-done.35.other, ...), custom_call_target="tpu_custom_call", output_to_operand_aliasing={{0}: (5, {}), {1}: (6, {})} | custom-call | flops 2097152 | bytes 5242880 | tf_op jit(solution)/shard_map/prepare/pallas_call | solution.py:104
  228.6 5.3 %prepare.24 = (bf16[17,2048,512]{2,1,0:T(8,128)(2,1)}, bf16[17,256,2048]{2,1,0:T(8,128)(2,1)}) custom-call(s32[2]{0:T(128)S(1)} %pad_add_fusion.16.meta, bf16[1024,512]{1,0:T(8,128)(2,1)} %collective-permute-done.18.mine, bf16[1024,512]{1,0:T(8,128)(2,1)} %collective-permute-done.34.other, ...), custom_call_target="tpu_custom_call", output_to_operand_aliasing={{0}: (5, {}), {1}: (6, {})} | custom-call | flops 2097152 | bytes 5242880 | tf_op jit(solution)/shard_map/prepare/pallas_call | solution.py:104
  233.9 4.5 %prepare.25 = (bf16[17,2048,512]{2,1,0:T(8,128)(2,1)}, bf16[17,256,2048]{2,1,0:T(8,128)(2,1)}) custom-call(s32[2]{0:T(128)S(1)} %pad_add_fusion.15.meta, bf16[1024,512]{1,0:T(8,128)(2,1)} %collective-permute-done.9.mine, bf16[1024,512]{1,0:T(8,128)(2,1)S(1)} %copy-done.25, ...), custom_call_target="tpu_custom_call", output_to_operand_aliasing={{0}: (5, {}), {1}: (6, {})} | custom-call | flops 2097152 | bytes 5242880 | tf_op jit(solution)/shard_map/prepare/pallas_call | solution.py:104
  238.4 4.5 %prepare.26 = (bf16[17,2048,512]{2,1,0:T(8,128)(2,1)}, bf16[17,256,2048]{2,1,0:T(8,128)(2,1)}) custom-call(s32[2]{0:T(128)S(1)} %pad_add_fusion.14.meta, bf16[1024,512]{1,0:T(8,128)(2,1)} %collective-permute-done.6.mine, bf16[1024,512]{1,0:T(8,128)(2,1)S(1)} %copy-done.23, ...), custom_call_target="tpu_custom_call", output_to_operand_aliasing={{0}: (5, {}), {1}: (6, {})} | custom-call | flops 2097152 | bytes 5242880 | tf_op jit(solution)/shard_map/prepare/pallas_call | solution.py:104
  242.8 4.4 %prepare.27 = (bf16[17,2048,512]{2,1,0:T(8,128)(2,1)}, bf16[17,256,2048]{2,1,0:T(8,128)(2,1)}) custom-call(s32[2]{0:T(128)S(1)} %pad_add_fusion.13.meta, bf16[1024,512]{1,0:T(8,128)(2,1)} %collective-permute-done.7.mine, bf16[1024,512]{1,0:T(8,128)(2,1)S(1)} %copy-done.27, ...), custom_call_target="tpu_custom_call", output_to_operand_aliasing={{0}: (5, {}), {1}: (6, {})} | custom-call | flops 2097152 | bytes 5242880 | tf_op jit(solution)/shard_map/prepare/pallas_call | solution.py:104
  247.8 11.6 %grams.5.rest_2_.rest_0_ = f32[34,256,512]{2,1,0:T(8,128)} custom-call(s32[34]{0:T(128)S(1)} %get-tuple-element.96.lefts, s32[34]{0:T(128)S(1)} %get-tuple-element.95.rights, s32[34]{0:T(128)S(1)} %get-tuple-element.94.slots, s32[34]{0:T(128)S(1)} %get-tuple-element.93.steps, s32[2]{0:T(128)S(1)} %pad_add_fusion.21.span, ...), custom_call_target="tpu_custom_call" | custom-call | flops 4294967296 | bytes 33554432 | tf_op jit(solution)/shard_map/grams/pallas_call | solution.py:162
  269.8 3.5 prepare.31
  273.3 3.5 prepare.32
  276.9 5.1 %prepare.33 = (bf16[17,2048,512]{2,1,0:T(8,128)(2,1)}, bf16[17,256,2048]{2,1,0:T(8,128)(2,1)}) custom-call(s32[2]{0:T(128)S(1)} %pad_add_fusion.7.meta, bf16[1024,512]{1,0:T(8,128)(2,1)S(1)} %collective-permute-done.10.mine, bf16[1024,512]{1,0:T(8,128)(2,1)} %collective-permute-done.23.other, ...), custom_call_target="tpu_custom_call", output_to_operand_aliasing={{0}: (5, {}), {1}: (6, {})} | custom-call | flops 2097152 | bytes 5242880 | tf_op jit(solution)/shard_map/prepare/pallas_call | solution.py:104
  282.5 11.4 %grams.6.rest_2_.rest_0_ = f32[34,256,512]{2,1,0:T(8,128)} custom-call(s32[34]{0:T(128)S(1)} %get-tuple-element.96.lefts, s32[34]{0:T(128)S(1)} %get-tuple-element.95.rights, s32[34]{0:T(128)S(1)} %get-tuple-element.94.slots, s32[34]{0:T(128)S(1)} %get-tuple-element.93.steps, s32[2]{0:T(128)S(1)} %pad_add_fusion.22.span, ...), custom_call_target="tpu_custom_call", output_to_operand_aliasing={{}: (8, {})} | custom-call | flops 4294967296 | bytes 33554432 | tf_op jit(solution)/shard_map/grams/pallas_call | solution.py:162
  294.0 5.3 %prepare.34 = (bf16[17,2048,512]{2,1,0:T(8,128)(2,1)}, bf16[17,256,2048]{2,1,0:T(8,128)(2,1)}) custom-call(s32[2]{0:T(128)S(1)} %pad_add_fusion.6.meta, bf16[1024,512]{1,0:T(8,128)(2,1)} %collective-permute-done.2.mine, bf16[1024,512]{1,0:T(8,128)(2,1)} %collective-permute-done.22.other, ...), custom_call_target="tpu_custom_call", output_to_operand_aliasing={{0}: (5, {}), {1}: (6, {})} | custom-call | flops 2097152 | bytes 5242880 | tf_op jit(solution)/shard_map/prepare/pallas_call | solution.py:104
  299.2 5.3 %prepare.35 = (bf16[17,2048,512]{2,1,0:T(8,128)(2,1)}, bf16[17,256,2048]{2,1,0:T(8,128)(2,1)}) custom-call(s32[2]{0:T(128)S(1)} %pad_add_fusion.5.meta, bf16[1024,512]{1,0:T(8,128)(2,1)} %collective-permute-done.20.mine, bf16[1024,512]{1,0:T(8,128)(2,1)} %collective-permute-done.21.other, ...), custom_call_target="tpu_custom_call", output_to_operand_aliasing={{0}: (5, {}), {1}: (6, {})} | custom-call | flops 2097152 | bytes 5242880 | tf_op jit(solution)/shard_map/prepare/pallas_call | solution.py:104
  304.5 12.0 %grams.7.rest_2_.rest_0_ = f32[34,256,512]{2,1,0:T(8,128)} custom-call(s32[34]{0:T(128)S(1)} %get-tuple-element.96.lefts, s32[34]{0:T(128)S(1)} %get-tuple-element.95.rights, s32[34]{0:T(128)S(1)} %get-tuple-element.94.slots, s32[34]{0:T(128)S(1)} %get-tuple-element.93.steps, s32[2]{0:T(128)S(1)} %pad_add_fusion.23.span, ...), custom_call_target="tpu_custom_call", output_to_operand_aliasing={{}: (8, {})} | custom-call | flops 4294967296 | bytes 33554432 | tf_op jit(solution)/shard_map/grams/pallas_call | solution.py:162
  316.5 5.3 %prepare.36 = (bf16[17,2048,512]{2,1,0:T(8,128)(2,1)}, bf16[17,256,2048]{2,1,0:T(8,128)(2,1)}) custom-call(s32[2]{0:T(128)S(1)} %pad_add_fusion.4.meta, bf16[1024,512]{1,0:T(8,128)(2,1)} %collective-permute-done.15.mine, bf16[1024,512]{1,0:T(8,128)(2,1)} %collective-permute-done.16.other, ...), custom_call_target="tpu_custom_call", output_to_operand_aliasing={{0}: (5, {}), {1}: (6, {})} | custom-call | flops 2097152 | bytes 5242880 | tf_op jit(solution)/shard_map/prepare/pallas_call | solution.py:104
  321.8 5.3 %prepare.37 = (bf16[17,2048,512]{2,1,0:T(8,128)(2,1)}, bf16[17,256,2048]{2,1,0:T(8,128)(2,1)}) custom-call(s32[2]{0:T(128)S(1)} %pad_add_fusion.3.meta, bf16[1024,512]{1,0:T(8,128)(2,1)} %collective-permute-done.11.mine, bf16[1024,512]{1,0:T(8,128)(2,1)} %collective-permute-done.14.other, ...), custom_call_target="tpu_custom_call", output_to_operand_aliasing={{0}: (5, {}), {1}: (6, {})} | custom-call | flops 2097152 | bytes 5242880 | tf_op jit(solution)/shard_map/prepare/pallas_call | solution.py:104
  327.1 12.3 %grams.8.rest_2_.rest_0_ = f32[34,256,512]{2,1,0:T(8,128)} custom-call(s32[34]{0:T(128)S(1)} %get-tuple-element.96.lefts, s32[34]{0:T(128)S(1)} %get-tuple-element.95.rights, s32[34]{0:T(128)S(1)} %get-tuple-element.94.slots, s32[34]{0:T(128)S(1)} %get-tuple-element.93.steps, s32[2]{0:T(128)S(1)} %pad_add_fusion.24.span, ...), custom_call_target="tpu_custom_call", output_to_operand_aliasing={{}: (8, {})} | custom-call | flops 4294967296 | bytes 33554432 | tf_op jit(solution)/shard_map/grams/pallas_call | solution.py:162
  339.4 5.3 %prepare.38 = (bf16[17,2048,512]{2,1,0:T(8,128)(2,1)}, bf16[17,256,2048]{2,1,0:T(8,128)(2,1)}) custom-call(s32[2]{0:T(128)S(1)} %pad_add_fusion.2.meta, bf16[1024,512]{1,0:T(8,128)(2,1)} %collective-permute-done.12.mine, bf16[1024,512]{1,0:T(8,128)(2,1)} %collective-permute-done.13.other, ...), custom_call_target="tpu_custom_call", output_to_operand_aliasing={{0}: (5, {}), {1}: (6, {})} | custom-call | flops 2097152 | bytes 5242880 | tf_op jit(solution)/shard_map/prepare/pallas_call | solution.py:104
  344.7 5.3 %prepare.39 = (bf16[17,2048,512]{2,1,0:T(8,128)(2,1)}, bf16[17,256,2048]{2,1,0:T(8,128)(2,1)}) custom-call(s32[2]{0:T(128)S(1)} %pad_add_fusion.1.meta, bf16[1024,512]{1,0:T(8,128)(2,1)} %collective-permute-done.3.mine, bf16[1024,512]{1,0:T(8,128)(2,1)} %collective-permute-done.4.other, ...), custom_call_target="tpu_custom_call", output_to_operand_aliasing={{0}: (5, {}), {1}: (6, {})} | custom-call | flops 2097152 | bytes 5242880 | tf_op jit(solution)/shard_map/prepare/pallas_call | solution.py:104
  350.0 12.4 %grams.9 = f32[34,256,512]{2,1,0:T(8,128)} custom-call(s32[34]{0:T(128)S(1)} %get-tuple-element.96.lefts, s32[34]{0:T(128)S(1)} %get-tuple-element.95.rights, s32[34]{0:T(128)S(1)} %get-tuple-element.94.slots, s32[34]{0:T(128)S(1)} %get-tuple-element.93.steps, s32[2]{0:T(128)S(1)} %pad_add_fusion.span, ...), custom_call_target="tpu_custom_call", output_to_operand_aliasing={{}: (8, {})} | custom-call | flops 4294967296 | bytes 33554432 | tf_op jit(solution)/shard_map/grams/pallas_call | solution.py:162
  (192 shorter events, 96.5 us)
Async XLA Ops:
  2.7 43.0 %collective-permute-start.38 = (bf16[1024,512]{1,0:T(8,128)(2,1)}, bf16[1024,512]{1,0:T(8,128)(2,1)}, u32[]{:S(2)}, u32[]{:S(2)}) collective-permute-start(bf16[1024,512]{1,0:T(8,128)(2,1)} %get-tuple-element.101.mine), channel_id=1, source_target_pairs={{0,1},{1,0},{2,3},{3,2},{4,5},{5,4},{6,7},{7,6},{8,9},{9,8},{10,11... | collective-permute-start | bytes 3145736 | tf_op jit(solution)/shard_map/ppermute | solution.py:248
  3.3 42.4 %collective-permute-start.37 = (bf16[1024,512]{1,0:T(8,128)(2,1)S(1)}, bf16[1024,512]{1,0:T(8,128)(2,1)}, u32[]{:S(2)}, u32[]{:S(2)}) collective-permute-start(bf16[1024,512]{1,0:T(8,128)(2,1)S(1)} %get-tuple-element.100.mine), channel_id=1, source_target_pairs={{0,1},{1,0},{2,3},{3,2},{4,5},{5,4},{6,7},{7,6},{8,9},{9,8},{10,11... | collective-permute-start | bytes 3145736 | tf_op jit(solution)/shard_map/ppermute | solution.py:248
  3.3 44.0 %collective-permute-start = (bf16[1024,512]{1,0:T(8,128)(2,1)}, bf16[1024,512]{1,0:T(8,128)(2,1)}, u32[]{:S(2)}, u32[]{:S(2)}) collective-permute-start(bf16[1024,512]{1,0:T(8,128)(2,1)} %get-tuple-element.101.mine), channel_id=1, source_target_pairs={{0,4},{2,6},{4,0},{6,2},{8,12},{10,14},{12,8},{14,10},{1,5},{3,7},... | collective-permute-start | bytes 3145736 | tf_op jit(solution)/shard_map/ppermute | solution.py:208
  4.6 44.3 %collective-permute-start.17 = (bf16[1024,512]{1,0:T(8,128)(2,1)}, bf16[1024,512]{1,0:T(8,128)(2,1)S(1)}, u32[]{:S(2)}, u32[]{:S(2)}) collective-permute-start(bf16[1024,512]{1,0:T(8,128)(2,1)} %get-tuple-element.101.mine), channel_id=1, source_target_pairs={{0,2},{2,0},{4,6},{6,4},{8,10},{10,8},{12,14},{14,12},{1,3},{3,1},... | collective-permute-start | bytes 3145736 | tf_op jit(solution)/shard_map/ppermute | solution.py:207
  45.7 24.5 %collective-permute-start.9 = (bf16[1024,512]{1,0:T(8,128)(2,1)S(1)}, bf16[1024,512]{1,0:T(8,128)(2,1)}, u32[]{:S(2)}, u32[]{:S(2)}) collective-permute-start(bf16[1024,512]{1,0:T(8,128)(2,1)S(1)} %get-tuple-element.100.mine), channel_id=1, source_target_pairs={{0,4},{2,6},{4,0},{6,2},{8,12},{10,14},{12,8},{14,10},{1,5},{3,7},... | collective-permute-start | bytes 3145736 | tf_op jit(solution)/shard_map/ppermute | solution.py:208
  45.7 37.4 %collective-permute-start.6 = (bf16[1024,512]{1,0:T(8,128)(2,1)S(1)}, bf16[1024,512]{1,0:T(8,128)(2,1)}, u32[]{:S(2)}, u32[]{:S(2)}) collective-permute-start(bf16[1024,512]{1,0:T(8,128)(2,1)S(1)} %get-tuple-element.100.mine), channel_id=1, source_target_pairs={{0,2},{2,0},{4,6},{6,4},{8,10},{10,8},{12,14},{14,12},{1,3},{3,1},... | collective-permute-start | bytes 3145736 | tf_op jit(solution)/shard_map/ppermute | solution.py:207
  47.3 35.8 %collective-permute-start.7 = (bf16[1024,512]{1,0:T(8,128)(2,1)S(1)}, bf16[1024,512]{1,0:T(8,128)(2,1)}, u32[]{:S(2)}, u32[]{:S(2)}) collective-permute-start(bf16[1024,512]{1,0:T(8,128)(2,1)S(1)} %get-tuple-element.100.mine), channel_id=1, source_target_pairs={{4,8},{6,10},{8,4},{10,6},{5,9},{7,11},{9,5},{11,7},{20,24},{22,26... | collective-permute-start | bytes 3145736 | tf_op jit(solution)/shard_map/ppermute | solution.py:209
  49.0 36.0 %collective-permute-start.36 = (bf16[1024,512]{1,0:T(8,128)(2,1)}, bf16[1024,512]{1,0:T(8,128)(2,1)}, u32[]{:S(2)}, u32[]{:S(2)}) collective-permute-start(bf16[1024,512]{1,0:T(8,128)(2,1)} %collective-permute-done.mine), channel_id=1, source_target_pairs={{0,1},{1,0},{2,3},{3,2},{4,5},{5,4},{6,7},{7,6},{8,9},{9,8},{10,11... | collective-permute-start | bytes 3145736 | tf_op jit(solution)/shard_map/ppermute | solution.py:248
  49.6 37.2 %collective-permute-start.35 = (bf16[1024,512]{1,0:T(8,128)(2,1)S(1)}, bf16[1024,512]{1,0:T(8,128)(2,1)}, u32[]{:S(2)}, u32[]{:S(2)}) collective-permute-start(bf16[1024,512]{1,0:T(8,128)(2,1)S(1)} %collective-permute-done.17.mine), channel_id=1, source_target_pairs={{0,1},{1,0},{2,3},{3,2},{4,5},{5,4},{6,7},{7,6},{8,9},{9,8},{10,11... | collective-permute-start | bytes 3145736 | tf_op jit(solution)/shard_map/ppermute | solution.py:248
  70.2 25.5 %collective-permute-start.34 = (bf16[1024,512]{1,0:T(8,128)(2,1)}, bf16[1024,512]{1,0:T(8,128)(2,1)}, u32[]{:S(2)}, u32[]{:S(2)}) collective-permute-start(bf16[1024,512]{1,0:T(8,128)(2,1)} %collective-permute-done.18.mine), channel_id=1, source_target_pairs={{0,1},{1,0},{2,3},{3,2},{4,5},{5,4},{6,7},{7,6},{8,9},{9,8},{10,11... | collective-permute-start | bytes 3145736 | tf_op jit(solution)/shard_map/ppermute | solution.py:248
  85.0 23.4 %collective-permute-start.31 = (bf16[1024,512]{1,0:T(8,128)(2,1)}, bf16[1024,512]{1,0:T(8,128)(2,1)S(1)}, u32[]{:S(2)}, u32[]{:S(2)}) collective-permute-start(bf16[1024,512]{1,0:T(8,128)(2,1)} %collective-permute-done.7.mine), channel_id=1, source_target_pairs={{0,1},{1,0},{2,3},{3,2},{4,5},{5,4},{6,7},{7,6},{8,9},{9,8},{10,11... | collective-permute-start | bytes 3145736 | tf_op jit(solution)/shard_map/ppermute | solution.py:248
  86.8 31.9 %collective-permute-start.19 = (bf16[1024,512]{1,0:T(8,128)(2,1)S(1)}, bf16[1024,512]{1,0:T(8,128)(2,1)S(1)}, u32[]{:S(2)}, u32[]{:S(2)}) collective-permute-start(bf16[1024,512]{1,0:T(8,128)(2,1)S(1)} %get-tuple-element.103), channel_id=1, source_target_pairs={{0,4},{2,6},{4,0},{6,2},{8,12},{10,14},{12,8},{14,10},{1,5},{3,7},... | collective-permute-start | bytes 3145736 | tf_op jit(solution)/shard_map/ppermute | solution.py:208
  95.6 24.1 %collective-permute-start.28 = (bf16[1024,512]{1,0:T(8,128)(2,1)S(1)}, bf16[1024,512]{1,0:T(8,128)(2,1)S(1)}, u32[]{:S(2)}, u32[]{:S(2)}) collective-permute-start(bf16[1024,512]{1,0:T(8,128)(2,1)S(1)} %get-tuple-element.102), channel_id=1, source_target_pairs={{0,2},{2,0},{4,6},{6,4},{8,10},{10,8},{12,14},{14,12},{1,3},{3,1},... | collective-permute-start | bytes 3145736 | tf_op jit(solution)/shard_map/ppermute | solution.py:207
  100.9 40.3 %collective-permute-start.8 = (bf16[1024,512]{1,0:T(8,128)(2,1)S(1)}, bf16[1024,512]{1,0:T(8,128)(2,1)S(1)}, u32[]{:S(2)}, u32[]{:S(2)}) collective-permute-start(bf16[1024,512]{1,0:T(8,128)(2,1)S(1)} %get-tuple-element.105), channel_id=1, source_target_pairs={{0,4},{2,6},{4,0},{6,2},{8,12},{10,14},{12,8},{14,10},{1,5},{3,7},... | collective-permute-start | bytes 3145736 | tf_op jit(solution)/shard_map/ppermute | solution.py:208
  101.9 29.1 %collective-permute-start.1 = (bf16[1024,512]{1,0:T(8,128)(2,1)}, bf16[1024,512]{1,0:T(8,128)(2,1)S(1)}, u32[]{:S(2)}, u32[]{:S(2)}) collective-permute-start(bf16[1024,512]{1,0:T(8,128)(2,1)} %collective-permute-done.mine), channel_id=1, source_target_pairs={{4,8},{6,10},{8,4},{10,6},{5,9},{7,11},{9,5},{11,7},{20,24},{22,26... | collective-permute-start | bytes 3145736 | tf_op jit(solution)/shard_map/ppermute | solution.py:209
  109.3 34.4 %collective-permute-start.24 = (bf16[1024,512]{1,0:T(8,128)(2,1)S(1)}, bf16[1024,512]{1,0:T(8,128)(2,1)S(1)}, u32[]{:S(2)}, u32[]{:S(2)}) collective-permute-start(bf16[1024,512]{1,0:T(8,128)(2,1)S(1)} %get-tuple-element.104), channel_id=1, source_target_pairs={{0,2},{2,0},{4,6},{6,4},{8,10},{10,8},{12,14},{14,12},{1,3},{3,1},... | collective-permute-start | bytes 3145736 | tf_op jit(solution)/shard_map/ppermute | solution.py:207
  118.7 26.0 %collective-permute-start.10 = (bf16[1024,512]{1,0:T(8,128)(2,1)}, bf16[1024,512]{1,0:T(8,128)(2,1)S(1)}, u32[]{:S(2)}, u32[]{:S(2)}) collective-permute-start(bf16[1024,512]{1,0:T(8,128)(2,1)} %collective-permute-done.9.mine), channel_id=1, source_target_pairs={{4,8},{6,10},{8,4},{10,6},{5,9},{7,11},{9,5},{11,7},{20,24},{22,26... | collective-permute-start | bytes 3145736 | tf_op jit(solution)/shard_map/ppermute | solution.py:209
  119.8 31.5 %collective-permute-start.30 = (bf16[1024,512]{1,0:T(8,128)(2,1)S(1)}, bf16[1024,512]{1,0:T(8,128)(2,1)S(1)}, u32[]{:S(2)}, u32[]{:S(2)}) collective-permute-start(bf16[1024,512]{1,0:T(8,128)(2,1)S(1)} %collective-permute-done.19.mine), channel_id=1, source_target_pairs={{0,1},{1,0},{2,3},{3,2},{4,5},{5,4},{6,7},{7,6},{8,9},{9,8},{10,11... | collective-permute-start | bytes 3145736 | tf_op jit(solution)/shard_map/ppermute | solution.py:248
  131.1 26.4 %collective-permute-start.29 = (bf16[1024,512]{1,0:T(8,128)(2,1)S(1)}, bf16[1024,512]{1,0:T(8,128)(2,1)S(1)}, u32[]{:S(2)}, u32[]{:S(2)}) collective-permute-start(bf16[1024,512]{1,0:T(8,128)(2,1)S(1)} %collective-permute-done.28.mine), channel_id=1, source_target_pairs={{0,1},{1,0},{2,3},{3,2},{4,5},{5,4},{6,7},{7,6},{8,9},{9,8},{10,11... | collective-permute-start | bytes 3145736 | tf_op jit(solution)/shard_map/ppermute | solution.py:248
  144.8 27.8 %collective-permute-start.2 = (bf16[1024,512]{1,0:T(8,128)(2,1)S(1)}, bf16[1024,512]{1,0:T(8,128)(2,1)}, u32[]{:S(2)}, u32[]{:S(2)}) collective-permute-start(bf16[1024,512]{1,0:T(8,128)(2,1)S(1)} %collective-permute-done.1.mine), channel_id=1, source_target_pairs={{0,4},{2,6},{4,0},{6,2},{8,12},{10,14},{12,8},{14,10},{1,5},{3,7},... | collective-permute-start | bytes 3145736 | tf_op jit(solution)/shard_map/ppermute | solution.py:208
  157.5 30.1 %collective-permute-start.11 = (bf16[1024,512]{1,0:T(8,128)(2,1)}, bf16[1024,512]{1,0:T(8,128)(2,1)}, u32[]{:S(2)}, u32[]{:S(2)}) collective-permute-start(bf16[1024,512]{1,0:T(8,128)(2,1)} %broadcast_select_fusion.4), channel_id=1, source_target_pairs={{0,2},{2,0},{4,6},{6,4},{8,10},{10,8},{12,14},{14,12},{1,3},{3,1},... | collective-permute-start | bytes 3145736 | tf_op jit(solution)/shard_map/ppermute | solution.py:207
  157.5 30.0 %collective-permute-start.23 = (bf16[1024,512]{1,0:T(8,128)(2,1)S(1)}, bf16[1024,512]{1,0:T(8,128)(2,1)}, u32[]{:S(2)}, u32[]{:S(2)}) collective-permute-start(bf16[1024,512]{1,0:T(8,128)(2,1)S(1)} %collective-permute-done.10.mine), channel_id=1, source_target_pairs={{0,1},{1,0},{2,3},{3,2},{4,5},{5,4},{6,7},{7,6},{8,9},{9,8},{10,11... | collective-permute-start | bytes 3145736 | tf_op jit(solution)/shard_map/ppermute | solution.py:248
  160.1 45.0 %collective-permute-start.20 = (bf16[1024,512]{1,0:T(8,128)(2,1)}, bf16[1024,512]{1,0:T(8,128)(2,1)}, u32[]{:S(2)}, u32[]{:S(2)}) collective-permute-start(bf16[1024,512]{1,0:T(8,128)(2,1)} %broadcast_select_fusion.2), channel_id=1, source_target_pairs={{0,2},{2,0},{4,6},{6,4},{8,10},{10,8},{12,14},{14,12},{1,3},{3,1},... | collective-permute-start | bytes 3145736 | tf_op jit(solution)/shard_map/ppermute | solution.py:207
  164.4 82.9 %collective-permute-start.15 = (bf16[1024,512]{1,0:T(8,128)(2,1)S(1)}, bf16[1024,512]{1,0:T(8,128)(2,1)}, u32[]{:S(2)}, u32[]{:S(2)}) collective-permute-start(bf16[1024,512]{1,0:T(8,128)(2,1)S(1)} %collective-permute-done.10.mine), channel_id=1, source_target_pairs={{0,4},{2,6},{4,0},{6,2},{8,12},{10,14},{12,8},{14,10},{1,5},{3,7},... | collective-permute-start | bytes 3145736 | tf_op jit(solution)/shard_map/ppermute | solution.py:208
  172.6 74.7 %collective-permute-start.22 = (bf16[1024,512]{1,0:T(8,128)(2,1)}, bf16[1024,512]{1,0:T(8,128)(2,1)}, u32[]{:S(2)}, u32[]{:S(2)}) collective-permute-start(bf16[1024,512]{1,0:T(8,128)(2,1)} %collective-permute-done.2.mine), channel_id=1, source_target_pairs={{0,1},{1,0},{2,3},{3,2},{4,5},{5,4},{6,7},{7,6},{8,9},{9,8},{10,11... | collective-permute-start | bytes 3145736 | tf_op jit(solution)/shard_map/ppermute | solution.py:248
  187.5 94.6 %collective-permute-start.3 = (bf16[1024,512]{1,0:T(8,128)(2,1)}, bf16[1024,512]{1,0:T(8,128)(2,1)}, u32[]{:S(2)}, u32[]{:S(2)}) collective-permute-start(bf16[1024,512]{1,0:T(8,128)(2,1)} %collective-permute-done.2.mine), channel_id=1, source_target_pairs={{0,2},{2,0},{4,6},{6,4},{8,10},{10,8},{12,14},{14,12},{1,3},{3,1},... | collective-permute-start | bytes 3145736 | tf_op jit(solution)/shard_map/ppermute | solution.py:207
  187.6 94.4 %collective-permute-start.12 = (bf16[1024,512]{1,0:T(8,128)(2,1)}, bf16[1024,512]{1,0:T(8,128)(2,1)}, u32[]{:S(2)}, u32[]{:S(2)}) collective-permute-start(bf16[1024,512]{1,0:T(8,128)(2,1)} %collective-permute-done.11.mine), channel_id=1, source_target_pairs={{0,4},{2,6},{4,0},{6,2},{8,12},{10,14},{12,8},{14,10},{1,5},{3,7},... | collective-permute-start | bytes 3145736 | tf_op jit(solution)/shard_map/ppermute | solution.py:208
  205.0 94.2 %collective-permute-start.21 = (bf16[1024,512]{1,0:T(8,128)(2,1)}, bf16[1024,512]{1,0:T(8,128)(2,1)}, u32[]{:S(2)}, u32[]{:S(2)}) collective-permute-start(bf16[1024,512]{1,0:T(8,128)(2,1)} %collective-permute-done.20.mine), channel_id=1, source_target_pairs={{0,1},{1,0},{2,3},{3,2},{4,5},{5,4},{6,7},{7,6},{8,9},{9,8},{10,11... | collective-permute-start | bytes 3145736 | tf_op jit(solution)/shard_map/ppermute | solution.py:248
  247.3 74.5 %collective-permute-start.14 = (bf16[1024,512]{1,0:T(8,128)(2,1)}, bf16[1024,512]{1,0:T(8,128)(2,1)}, u32[]{:S(2)}, u32[]{:S(2)}) collective-permute-start(bf16[1024,512]{1,0:T(8,128)(2,1)} %collective-permute-done.11.mine), channel_id=1, source_target_pairs={{0,1},{1,0},{2,3},{3,2},{4,5},{5,4},{6,7},{7,6},{8,9},{9,8},{10,11... | collective-permute-start | bytes 3145736 | tf_op jit(solution)/shard_map/ppermute | solution.py:248
  247.3 69.1 %collective-permute-start.16 = (bf16[1024,512]{1,0:T(8,128)(2,1)}, bf16[1024,512]{1,0:T(8,128)(2,1)}, u32[]{:S(2)}, u32[]{:S(2)}) collective-permute-start(bf16[1024,512]{1,0:T(8,128)(2,1)} %collective-permute-done.15.mine), channel_id=1, source_target_pairs={{0,1},{1,0},{2,3},{3,2},{4,5},{5,4},{6,7},{7,6},{8,9},{9,8},{10,11... | collective-permute-start | bytes 3145736 | tf_op jit(solution)/shard_map/ppermute | solution.py:248
  282.0 57.4 %collective-permute-start.13 = (bf16[1024,512]{1,0:T(8,128)(2,1)}, bf16[1024,512]{1,0:T(8,128)(2,1)}, u32[]{:S(2)}, u32[]{:S(2)}) collective-permute-start(bf16[1024,512]{1,0:T(8,128)(2,1)} %collective-permute-done.12.mine), channel_id=1, source_target_pairs={{0,1},{1,0},{2,3},{3,2},{4,5},{5,4},{6,7},{7,6},{8,9},{9,8},{10,11... | collective-permute-start | bytes 3145736 | tf_op jit(solution)/shard_map/ppermute | solution.py:248
  282.1 62.6 %collective-permute-start.4 = (bf16[1024,512]{1,0:T(8,128)(2,1)}, bf16[1024,512]{1,0:T(8,128)(2,1)}, u32[]{:S(2)}, u32[]{:S(2)}) collective-permute-start(bf16[1024,512]{1,0:T(8,128)(2,1)} %collective-permute-done.3.mine), channel_id=1, source_target_pairs={{0,1},{1,0},{2,3},{3,2},{4,5},{5,4},{6,7},{7,6},{8,9},{9,8},{10,11... | collective-permute-start | bytes 3145736 | tf_op jit(solution)/shard_map/ppermute | solution.py:248
  (36 other events, 625.6 us)
